TPU v7x, 256 devices: a whole 4x4x8 slice. The times are simulated.
256 devices in a mesh: leaf: 64 (over z, x, core), rhs: 4 (over y).
Axes of the slice: x: 4, y: 4, z: 8, core: 2. Of those that a mesh axis runs over, the one named last changes fastest.
Arguments:
- density: bfloat16 [16, 512, 384], P('rhs', 'leaf'), may hold values from -6 to 6
- near_blocks: bfloat16 [512, 16, 384, 384], P('leaf', 'rhs'), may hold values from -0.078125 to 0.078125
- near_send: int32 [64, 64, 1], P('leaf'), may hold values from 0 to 7, as said below
- near_slot: int32 [512, 16], P('leaf', 'rhs'), may hold values from 0 to 71, as said below
- col_basis: bfloat16 [512, 64, 384], P('leaf'), may hold values from -0.3125 to 0.3125
- up_transfer: bfloat16 [384, 64, 128], P('leaf'), may hold values from -0.5 to 0.5
- coupling: bfloat16 [896, 64, 1024], P('leaf', None, 'rhs'), may hold values from -0.1875 to 0.1875
- down_transfer: bfloat16 [384, 64, 128], P('leaf'), may hold values from -0.75 to 0.75
- row_basis: bfloat16 [512, 64, 384], P('leaf'), may hold values from -0.75 to 0.75
- coup_send: int32 [64, 64, 1], P('leaf'), may hold values from 0 to 13, as said below
- coup_slot: int32 [896, 16], P('leaf', 'rhs'), may hold values from 0 to 77, as said below
Outputs:
- velocity: bfloat16 [16, 512, 384], P('rhs', 'leaf')
Inputs may be any that keep to these rules, and one draw needn't show every extreme that they name: `near_send`: entry [s, r, k] is a leaf of device s, numbered within s; for each s and r the 1 entries differ. `near_slot`: entry of device r's table: below 8 its own leaf of that number, else value - 8 = m names device m, and the entry stands for its leaf near_send[m, r, 0]. `coup_send`: entry [s, r, k] is a cluster of device s, numbered within s; for each s and r the 1 entries differ and have one level. `coup_slot`: entry of device r's table: below 14 its own cluster of that number, else value - 14 = m names device m, and the entry stands for its cluster coup_send[m, r, 0]; it has the same level as the row's cluster.
All inputs are finite; a program needn't handle non-finite values.
Results may differ from a plain program's by a relative error of at most 0.0056.
Values may be sent and summed in bfloat16 or wider, within the bound.
A program may use at most 64 MiB of HBM per device.

v0:
```python
import jax
import jax.numpy as jnp
from jax import lax
from jax.sharding import PartitionSpec as P

HIGHEST_PRECISION = lax.Precision.HIGHEST


def upward(fields, col_basis, up_transfer):
    leaves = col_basis.shape[0]
    rank_size = col_basis.shape[1]
    half_count = leaves // 2
    quarter = leaves // 4
    width = fields.shape[0]
    fine_charges = jnp.einsum(
        "lru,slu->lrs", col_basis, fields, preferred_element_type=jnp.float32
    ).astype(jnp.bfloat16)
    mid_charges = jnp.einsum(
        "prc,pcs->prs",
        up_transfer[:half_count],
        fine_charges.reshape(half_count, 2 * rank_size, width),
        preferred_element_type=jnp.float32,
    ).astype(jnp.bfloat16)
    top_charges = jnp.einsum(
        "prc,pcs->prs",
        up_transfer[half_count:],
        mid_charges.reshape(quarter, 2 * rank_size, width),
        preferred_element_type=jnp.float32,
    ).astype(jnp.bfloat16)
    return jnp.concatenate([fine_charges, mid_charges, top_charges], axis=0)


def near_outbox(fields, near_send):
    peer_count = near_send.shape[1]
    per_peer = near_send.shape[2]
    picked = jnp.take(fields, near_send[0].reshape(-1), axis=1)
    return picked.reshape(fields.shape[0], peer_count, per_peer, fields.shape[2])


def far_outbox(charges, coup_send):
    peer_count = coup_send.shape[1]
    per_peer = coup_send.shape[2]
    picked = jnp.take(charges, coup_send[0].reshape(-1), axis=0)
    return picked.reshape(peer_count, per_peer, charges.shape[1], charges.shape[2])


def build_tables(fields, charges, arrived, landed):
    near_lookup = jnp.concatenate(
        [fields, arrived.reshape(arrived.shape[0], -1, arrived.shape[3])], axis=1
    )
    far_lookup = jnp.concatenate(
        [charges, landed.reshape(-1, landed.shape[2], landed.shape[3])], axis=0
    )
    return (near_lookup, far_lookup)


def near_field(near_lookup, near_blocks, near_slot):
    width = near_lookup.shape[0]
    leaves = near_slot.shape[0]
    columns = near_slot.shape[1]
    gathered = jnp.take(near_lookup, near_slot.reshape(-1), axis=1).reshape(
        width, leaves, columns, near_lookup.shape[2]
    )
    return jnp.einsum("lkvu,slku->slv", near_blocks, gathered, preferred_element_type=jnp.float32)


def far_field(far_lookup, coupling, coup_slot, down_transfer, row_basis):
    clusters = coup_slot.shape[0]
    columns = coup_slot.shape[1]
    rank_size = far_lookup.shape[1]
    width = far_lookup.shape[2]
    leaves = row_basis.shape[0]
    half_count = leaves // 2
    picked = jnp.take(far_lookup, coup_slot.reshape(-1), axis=0).reshape(
        clusters, columns * rank_size, width
    )
    coupled = jnp.einsum("grc,gcs->grs", coupling, picked, preferred_element_type=jnp.float32)
    down_wide = down_transfer.astype(jnp.float32)
    coarse = coupled[leaves + half_count :]
    middle = coupled[leaves : leaves + half_count] + jnp.einsum(
        "prc,prs->pcs", down_wide[half_count:], coarse, precision=HIGHEST_PRECISION
    ).reshape(half_count, rank_size, width)
    finest = coupled[:leaves] + jnp.einsum(
        "prc,prs->pcs", down_wide[:half_count], middle, precision=HIGHEST_PRECISION
    ).reshape(leaves, rank_size, width)
    return jnp.einsum(
        "lru,lrs->slu", row_basis.astype(jnp.float32), finest, precision=HIGHEST_PRECISION
    )


def shards(
    density,
    near_blocks,
    near_send,
    near_slot,
    col_basis,
    up_transfer,
    coupling,
    down_transfer,
    row_basis,
    coup_send,
    coup_slot,
):
    fields = lax.all_gather(density, "rhs", axis=0, tiled=True)
    charges = upward(fields, col_basis, up_transfer)
    arrived = lax.all_to_all(
        near_outbox(fields, near_send), "leaf", split_axis=1, concat_axis=1, tiled=True
    )
    landed = lax.all_to_all(
        far_outbox(charges, coup_send), "leaf", split_axis=0, concat_axis=0, tiled=True
    )
    near_lookup, far_lookup = build_tables(fields, charges, arrived, landed)
    partial_value = near_field(near_lookup, near_blocks, near_slot) + far_field(
        far_lookup, coupling, coup_slot, down_transfer, row_basis
    )
    return lax.psum_scatter(partial_value, "rhs", scatter_dimension=0, tiled=True).astype(
        jnp.bfloat16
    )


def solution(mesh):
    placed = (
        P("rhs", "leaf", None),
        P("leaf", "rhs", None, None),
        P("leaf", None, None),
        P("leaf", "rhs"),
        P("leaf", None, None),
        P("leaf", None, None),
        P("leaf", None, "rhs"),
        P("leaf", None, None),
        P("leaf", None, None),
        P("leaf", None, None),
        P("leaf", "rhs"),
    )
    return jax.shard_map(
        shards, mesh=mesh, in_specs=placed, out_specs=P("rhs", "leaf", None), check_vma=False
    )
```

profile of v0, /device:TPU:32, one launch (start us, length us, event | category | flops | bytes accessed | tf_op | source)
XLA Modules:
  0.0 112.6 jit_solution(3152465441245861847)
XLA Ops:
  6.5 0.7 fusion.19
  7.3 0.7 compare_and_fusion
  7.9 12.6 %all_gather.3 = bf16[16,8,384]{2,1,0:T(8,128)(2,1)S(1)} all-gather(bf16[4,8,384]{2,1,0:T(8,128)(2,1)} %param.11), channel_id=1, replica_groups=mesh['leaf'=64,'rhs'=4] {'rhs'}, dimensions={0}, use_global_device_ids=true | all-gather | bytes 122880 | tf_op jit(solution)/shard_map/all_gather | solution.py:104
  20.6 1.2 %convolution_convert_fusion = bf16[8,64,16]{1,2,0:T(8,128)(2,1)S(1)} fusion(bf16[8,64,384]{2,1,0:T(8,128)(2,1)} %param.15, bf16[16,8,384]{2,1,0:T(8,128)(2,1)S(1)} %all_gather.3), kind=kOutput, calls=%fused_computation.8 | convolution fusion | flops 6299648 | bytes 507904 | tf_op jit(solution)/shard_map/lru,slu->lrs/dot_general | solution.py:15
  21.8 0.1 reshape.186
  21.9 1.0 fusion.1
  22.9 0.1 reshape.187
  23.0 0.9 fusion.2
  23.9 0.6 gather_fusion.2
  24.6 0.1 fusion.23
  24.7 0.9 reshape.225
  25.6 11.6 %all-to-all-start.1 = ((bf16[64,2,512]{2,1,0:T(2,128)(2,1)}), bf16[64,2,512]{2,1,0:T(2,128)(2,1)S(1)}, u32[]{:S(2)}, u32[]{:S(2)}) async-start(bf16[64,2,512]{2,1,0:T(2,128)(2,1)} %reshape.225), calls=%async_computation.1 | async-start | bytes 262144 | tf_op jit(solution)/shard_map/all_to_all | solution.py:109
  37.2 0.7 fusion.17
  37.9 0.7 compare_and_fusion.2
  38.5 0.8 copy.57
  39.3 0.7 compare_and_fusion.3
  40.0 0.8 copy.65
  40.7 0.7 compare_and_fusion.1
  41.4 0.1 reshape.185
  41.5 0.1 reshape.189
  41.6 0.7 gather_fusion
  42.3 1.1 fusion.3
  43.4 4.0 %all-to-all-done.1 = bf16[64,2,512]{2,1,0:T(2,128)(2,1)S(1)} async-done(((bf16[64,2,512]{2,1,0:T(2,128)(2,1)}), bf16[64,2,512]{2,1,0:T(2,128)(2,1)S(1)}, u32[]{:S(2)}, u32[]{:S(2)}) %all-to-all-start.1) | async-done | bytes 131104 | tf_op jit(solution)/shard_map/all_to_all | solution.py:109
  47.4 6.3 %all-to-all-start = ((bf16[16,64,1,384]{3,0,2,1:T(8,128)(2,1)}), bf16[16,64,1,384]{3,0,2,1:T(8,128)(2,1)S(1)}, u32[]{:S(2)}, u32[]{:S(2)}) async-start(bf16[16,64,1,384]{3,0,2,1:T(8,128)(2,1)} %fusion.3), calls=%async_computation | async-start | bytes 1572864 | tf_op jit(solution)/shard_map/all_to_all | solution.py:106
  53.7 0.0 reduce-scatter.2.cloned.1.call-start
  53.8 0.1 copy.53
  53.9 0.1 copy.58
  54.0 0.1 broadcast_in_dim.48
  54.0 0.1 broadcast_in_dim.49
  54.2 0.2 reshape.226
  54.4 0.1 pad_maximum_fusion.1
  54.5 0.6 gather_fusion.3
  55.1 0.1 copy.66
  55.2 0.2 gather.31
  55.4 0.2 convolution_bitcast_fusion.1
  55.6 0.2 convolution_bitcast_fusion.3
  55.8 0.1 reshape.190
  55.9 0.2 convolution_bitcast_fusion.2
  56.1 0.1 reshape.191
  56.2 19.8 %all-to-all-done = bf16[16,64,1,384]{3,0,2,1:T(8,128)(2,1)S(1)} async-done(((bf16[16,64,1,384]{3,0,2,1:T(8,128)(2,1)}), bf16[16,64,1,384]{3,0,2,1:T(8,128)(2,1)S(1)}, u32[]{:S(2)}, u32[]{:S(2)}) %all-to-all-start) | async-done | bytes 786464 | tf_op jit(solution)/shard_map/all_to_all | solution.py:106
  76.0 0.1 pad_maximum_fusion
  76.1 0.6 gather_fusion.1
  76.8 6.2 %convolution_bitcast_fusion = f32[8,16,384]{2,1,0:T(8,128)S(1)} fusion(bf16[8,4,384,384]{3,2,1,0:T(8,128)(2,1)} %param.12, bf16[16,8,4,384]{3,0,2,1:T(8,128)(2,1)S(1)} %bitcast.75, pred[8,4]{1,0:T(8,128)(4,1)S(1)} %copy.53), kind=kOutput, calls=%fused_computation.6 | convolution fusion | flops 151191552 | bytes 10027040 | tf_op jit(solution)/shard_map/lkvu,slku->slv/dot_general | solution.py:64
  83.0 0.4 fusion
  83.4 0.7 copy.72
  84.1 0.0 reduce-scatter.2.cloned.1.call-update
  84.1 20.2 %reduce-scatter.2.cloned.1.call-done = f32[4,8,384]{2,1,0:T(8,128)} async-done(((f32[16,8,384]{2,1,0:T(8,128)}), f32[4,8,384]{2,1,0:T(8,128)}) %reduce-scatter.2.cloned.1.call-update) | async-done | bytes 49168 | tf_op jit(solution)/shard_map/reduce_scatter | solution.py:116
  104.4 1.4 %convert_element_type.25 = bf16[4,8,384]{2,1,0:T(8,128)(2,1)} convert(f32[4,8,384]{2,1,0:T(8,128)} %reduce-scatter.2.cloned.1.call-done) | non-fusion elementwise | flops 12288 | bytes 73728 | tf_op jit(solution)/shard_map/convert_element_type | solution.py:116
  (20 shorter events, 0.2 us)
Async XLA Ops:
  6.5 48.9 %copy-start = (bf16[14,64,256]{2,1,0:T(8,128)(2,1)S(1)}, bf16[14,64,256]{2,1,0:T(8,128)(2,1)}, u32[]{:S(2)}) copy-start(bf16[14,64,256]{2,1,0:T(8,128)(2,1)} %param.17) | copy-start | bytes 1376260
  6.5 49.1 %copy-start.2 = (bf16[6,64,128]{2,1,0:T(8,128)(2,1)S(1)}, bf16[6,64,128]{2,1,0:T(8,128)(2,1)}, u32[]{:S(2)}) copy-start(bf16[6,64,128]{2,1,0:T(8,128)(2,1)} %param.18) | copy-start | bytes 294916
  25.6 21.8 %all-to-all-start.1 = ((bf16[64,2,512]{2,1,0:T(2,128)(2,1)}), bf16[64,2,512]{2,1,0:T(2,128)(2,1)S(1)}, u32[]{:S(2)}, u32[]{:S(2)}) async-start(bf16[64,2,512]{2,1,0:T(2,128)(2,1)} %reshape.225), calls=%async_computation.1 | async-start | bytes 262144 | tf_op jit(solution)/shard_map/all_to_all | solution.py:109
  47.4 28.7 %all-to-all-start = ((bf16[16,64,1,384]{3,0,2,1:T(8,128)(2,1)}), bf16[16,64,1,384]{3,0,2,1:T(8,128)(2,1)S(1)}, u32[]{:S(2)}, u32[]{:S(2)}) async-start(bf16[16,64,1,384]{3,0,2,1:T(8,128)(2,1)} %fusion.3), calls=%async_computation | async-start | bytes 1572864 | tf_op jit(solution)/shard_map/all_to_all | solution.py:106
  53.7 50.7 %reduce-scatter.2.cloned.1.call-start = ((), (), s32[]{:S(2)}) async-start(), calls=%async_computation.3 | async-start | bytes 245760 | tf_op jit(solution)/shard_map/reduce_scatter | solution.py:116
  76.1 6.9 %copy-start.1 = (bf16[8,64,384]{2,1,0:T(8,128)(2,1)S(1)}, bf16[8,64,384]{2,1,0:T(8,128)(2,1)}, u32[]{:S(2)}) copy-start(bf16[8,64,384]{2,1,0:T(8,128)(2,1)} %param.19) | copy-start | bytes 1179652
Sparse Core Ops, SparseCore 0:
  84.3 20.0 reduce-scatter.1
where the time goes:
time: 114 us; the launch traced here: 113 us
  waiting for transfers between devices  44 us (39%)
  starting transfers between devices  18 us (16%)
  between operations  13.6 us (12%)
  blocking collectives  12.6 us (11%)
  matrix products  10.2 us (9%)
  local copies, waits for them, and re-layouts  7.24 us (6%)
  other arithmetic  6.92 us (6%)
    reduce_scatter x1, waiting for transfers between devices, shards(): lax.psum_scatter(partial_value, 'rhs', scatter_dimension=0, tiled=True)  20.2 us
    all_to_all x1, waiting for transfers between devices, shards(): lax.all_to_all(near_outbox(fields, near_send), 'leaf', split_axis=1, conc...  19.8 us
    all_gather x1, blocking collectives, shards(): fields = lax.all_gather(density, 'rhs', axis=0, tiled=True)  12.6 us
    all_to_all x1, starting transfers between devices, shards(): lax.all_to_all(far_outbox(charges, coup_send), 'leaf', split_axis=0, conc...  11.6 us
    all_to_all x1, starting transfers between devices, shards(): lax.all_to_all(near_outbox(fields, near_send), 'leaf', split_axis=1, conc...  6.33 us
    dot_general x1, matrix products, near_field(): jnp.einsum('lkvu,slku->slv', near_blocks, gathered, preferred_element_typ...  6.25 us
    all_to_all x1, waiting for transfers between devices, shards(): lax.all_to_all(far_outbox(charges, coup_send), 'leaf', split_axis=0, conc...  3.97 us
    unnamed x10, local copies, waits for them, and re-layouts  2.61 us
  transfers between devices with their start and end apart: 3, of which 3 were waited for; matrix products, arithmetic and copies ran while one was open for 8% of the time, Pallas kernels for 0%

commit v1 on v0

v1 whole, which is shorter than its diff:
```python
import functools

import jax
import jax.numpy as jnp
from jax import lax
from jax.experimental import pallas as pl
from jax.experimental.pallas import tpu as pltpu
from jax.sharding import PartitionSpec as P

BF = jnp.bfloat16
F32 = jnp.float32
MESH = pl.DeviceIdType.MESH
NT = (((1,), (1,)), ((), ()))
NN = (((1,), (0,)), ((), ()))
ORDER = (12, 13, 8, 9, 10, 11, 0, 1, 2, 3, 4, 5, 6, 7)
CHUNKS = 4
PER = 32 // CHUNKS


def dot(a, b, dims=NN):
    return lax.dot_general(a, b, dims, preferred_element_type=F32)


def iota(shape, axis):
    return lax.broadcasted_iota(jnp.int32, shape, axis)


def kernel(
    n_leaf,
    near_send,
    coup_send,
    near_slot,
    coup_slot,
    density_h,
    near_h,
    col_h,
    up_h,
    coupling_h,
    down_h,
    row_h,
    out,
    density,
    near,
    col,
    up,
    coupling,
    down,
    row,
    slots,
    slots_s,
    tiles,
    charges,
    table,
    send1,
    send2,
    recv2,
    send4,
    recv4,
    in_sem,
    near_sem,
    smem_sem,
    s0_send,
    s0_recv,
    s1_send,
    s1_recv,
    s2_send,
    s2_recv,
    s4_send,
    s4_recv,
):
    me = lax.axis_index("leaf")
    y = lax.axis_index("rhs")
    slow = ((density_h, density), (col_h, col), (up_h, up), (coupling_h, coupling), (down_h, down), (row_h, row))
    loads = [pltpu.make_async_copy(a, b, in_sem.at[i]) for i, (a, b) in enumerate(slow)]
    for load in loads:
        load.start()
    blocks = [pltpu.make_async_copy(near_h.at[i], near.at[i], near_sem.at[i]) for i in range(8)]
    for load in blocks:
        load.start()

    barrier = pltpu.get_barrier_semaphore()

    def greet(j, _):
        pl.semaphore_signal(
            barrier, inc=1, device_id={"leaf": lax.rem(me + j, n_leaf)}, device_id_type=MESH
        )
        return 0

    lax.fori_loop(1, n_leaf, greet, 0)
    for e in range(1, 4):
        pl.semaphore_signal(barrier, inc=1, device_id={"rhs": lax.rem(y + e, 4)}, device_id_type=MESH)

    slots[0, :, :] = jnp.zeros((8, 128), jnp.int32)
    slots[0, 0:4, 0:8] = near_slot[...]
    slots[0, 4:8, 0:14] = coup_slot[...]

    for load in loads[:3]:
        load.wait()
    flat = density[...].reshape(32, 384)
    stacked = jnp.concatenate([flat[:, 128 * c : 128 * c + 128] for c in range(3)], axis=0)
    r, q = iota((128, 96), 0), iota((128, 96), 1)
    pick = (r % 16 < 12) & (q == (r % 16) // 4 * 32 + r % 4 * 8 + r // 16)
    tile = dot(jnp.where(pick, 1.0, 0.0).astype(BF), stacked).astype(BF)
    r, q = iota((128, 32), 0), iota((128, 32), 1)
    pick = (r % 16 >= 12) & (q == r % 4 * 8 + r // 16)
    low = dot(jnp.where(pick, 1.0, 0.0).astype(BF), flat).astype(BF)
    left = iota((16, 128), 1) < 64

    def twice(a):
        return jnp.concatenate([a, a], axis=0)

    level = [dot(low[16 * i : 16 * i + 16], twice(col[i]), NT) for i in range(8)]
    values = [a.astype(BF) for a in level]
    for base, count in ((0, 4), (4, 2)):
        level = [
            dot(
                jnp.where(left, level[2 * j].astype(BF).astype(F32), level[2 * j + 1].astype(BF).astype(F32)).astype(BF),
                twice(up[base + j]),
                NT,
            )
            for j in range(count)
        ]
        values += [a.astype(BF) for a in level]
    for i in range(14):
        charges[i] = values[i]
        if i < 8:
            tiles[i] = tile[16 * i : 16 * i + 16]
            table[i] = tile[16 * i : 16 * i + 16] + values[i]
        else:
            table[i] = values[i]

    pl.semaphore_wait(barrier, n_leaf + 2)

    slot_copies = [
        pltpu.make_async_remote_copy(
            slots.at[0],
            slots.at[e],
            s0_send.at[e - 1],
            s0_recv.at[e - 1],
            device_id={"rhs": lax.rem(y + e, 4)},
            device_id_type=MESH,
        )
        for e in range(1, 4)
    ]
    for copy in slot_copies:
        copy.start()

    def listed(peer):
        return tiles[near_send[0, 0, peer]] + charges[coup_send[0, 0, peer]]

    def post(j, _):
        peer = lax.rem(me + j, n_leaf)
        send1[peer] = listed(peer)
        pltpu.make_async_remote_copy(
            send1.at[peer],
            table.at[14 + me],
            s1_send,
            s1_recv,
            device_id={"leaf": peer},
            device_id_type=MESH,
        ).start()
        return 0

    lax.fori_loop(1, n_leaf, post, 0)
    table[14 + me] = listed(me)

    for copy in slot_copies:
        copy.wait_recv()
    to_smem = pltpu.make_async_copy(slots, slots_s, smem_sem)
    to_smem.start()
    to_smem.wait()

    everything = pltpu.make_async_remote_copy(
        send1.at[pl.ds(0, n_leaf - 1)],
        table.at[pl.ds(14, n_leaf - 1)],
        s1_send,
        s1_recv,
        device_id={"leaf": lax.rem(me + 1, n_leaf)},
        device_id_type=MESH,
    )
    everything.wait_recv()

    rows, lanes = iota((16, 128), 0), iota((16, 128), 1)
    mask_n = jnp.where(rows < 12, 1.0, 0.0).astype(BF)
    mask_a = jnp.where((rows >= 12) & (lanes < 64), 1.0, 0.0).astype(BF)
    mask_b = jnp.where((rows >= 12) & (lanes >= 64), 1.0, 0.0).astype(BF)

    def read(e, i):
        slot = slots_s[e, i % 4, i // 4]
        value = table[slot + jnp.where(slot >= 8, 6, 0)] * mask_n
        if i < 28:
            g, k = ORDER[i // 2], i % 2 * 2
            value += table[slots_s[e, 4 + k, g]] * mask_a + table[slots_s[e, 5 + k, g]] * mask_b
        return value

    sends = []
    for chunk in range(CHUNKS):
        span = pl.ds(chunk * PER, PER)
        for e in (2, 1, 3):
            for i in range(chunk * PER, chunk * PER + PER):
                send2[e - 1, i] = read(4 - e, i)
            copy = pltpu.make_async_remote_copy(
                send2.at[e - 1, span],
                recv2.at[e, span],
                s2_send.at[e - 1, chunk],
                s2_recv.at[e - 1, chunk],
                device_id={"rhs": lax.rem(y + e, 4)},
                device_id_type=MESH,
            )
            copy.start()
            sends.append(copy)
        for i in range(chunk * PER, chunk * PER + PER):
            recv2[0, i] = read(0, i)

    for load in loads[3:]:
        load.wait()

    top = iota((8, 128), 0) < 4

    def regroup(i):
        parts = [recv2[e, i].astype(F32) for e in range(4)]
        groups = []
        for h in (0, 8):
            x = [p[h : h + 8] for p in parts]
            z = [pltpu.roll(p, 4, 0) for p in x]
            groups.append([jnp.where(top, x[0], z[1]), jnp.where(top, x[2], z[3])])
            groups.append([jnp.where(top, z[0], x[1]), jnp.where(top, z[2], x[3])])
        return [jnp.concatenate(g, axis=0).astype(BF) for g in groups]

    total = [None] * 8
    field = {}
    for chunk in range(CHUNKS):
        for copy in sends[3 * chunk : 3 * chunk + 3]:
            copy.wait_recv()
        pairs = {}
        for leaf in range(chunk * PER // 4, chunk * PER // 4 + PER // 4):
            blocks[leaf].wait()
            value = None
            for k in range(4):
                g = regroup(4 * leaf + k)
                pairs[4 * leaf + k] = g[3]
                part = dot(jnp.concatenate(g[:3], axis=1), near[leaf, k], NT)
                value = part if value is None else value + part
            total[leaf] = value
        for i in pairs:
            if i < 28 and i % 2 == 0:
                g = ORDER[i // 2]
                field[g] = dot(jnp.concatenate([pairs[i], pairs[i + 1]], axis=1), coupling[g], NT)

    def gain(parent, index):
        return dot(field[parent].astype(BF), down[index])

    for base, children, count, first in ((12, 8, 2, 4), (8, 0, 4, 0)):
        for j in range(count):
            both = gain(base + j, first + j)
            field[children + 2 * j] += both[:, :64]
            field[children + 2 * j + 1] += both[:, 64:]
    whole = jnp.concatenate(
        [(total[i] + dot(field[i].astype(BF), row[i])).astype(BF) for i in range(8)], axis=0
    )
    r, q = iota((128, 128), 0), iota((128, 128), 1)
    pick = q == r % 8 * 16 + r // 32 * 4 + r // 8 % 4
    sorted_rows = dot(jnp.where(pick, 1.0, 0.0).astype(BF), whole)
    last = []
    for e in range(1, 4):
        send4[e - 1] = sorted_rows[32 * e : 32 * e + 32].astype(BF)
        copy = pltpu.make_async_remote_copy(
            send4.at[e - 1],
            recv4.at[3 - e],
            s4_send.at[e - 1],
            s4_recv.at[3 - e],
            device_id={"rhs": lax.rem(y + 4 - e, 4)},
            device_id_type=MESH,
        )
        copy.start()
        last.append(copy)
    for copy in last:
        copy.wait()
    result = sorted_rows[:32]
    for e in range(3):
        result += recv4[e].astype(F32)
    out[...] = result.astype(BF).reshape(4, 8, 384)

    for copy in slot_copies:
        copy.wait_send()
    everything.wait_send()
    for copy in sends:
        copy.wait_send()


def shards(n_leaf, density, near_blocks, near_send, near_slot, col, up, coupling, down, row, coup_send, coup_slot):
    smem = pl.BlockSpec(memory_space=pltpu.SMEM)
    vmem = pl.BlockSpec(memory_space=pltpu.VMEM)
    hbm = pl.BlockSpec(memory_space=pl.ANY)
    big = [density, near_blocks, col, up, coupling, down, row]
    dma = pltpu.SemaphoreType.DMA
    return pl.pallas_call(
        functools.partial(kernel, n_leaf),
        out_shape=jax.ShapeDtypeStruct((4, 8, 384), BF),
        in_specs=[smem, smem, vmem, vmem] + [hbm] * len(big),
        out_specs=vmem,
        scratch_shapes=[pltpu.VMEM(a.shape, a.dtype) for a in big]
        + [
            pltpu.VMEM((4, 8, 128), jnp.int32),
            pltpu.SMEM((4, 8, 128), jnp.int32),
            pltpu.VMEM((8, 16, 128), BF),
            pltpu.VMEM((14, 16, 128), BF),
            pltpu.VMEM((14 + n_leaf, 16, 128), BF),
            pltpu.VMEM((n_leaf, 16, 128), BF),
            pltpu.VMEM((3, 32, 16, 128), BF),
            pltpu.VMEM((4, 32, 16, 128), BF),
            pltpu.VMEM((3, 32, 384), BF),
            pltpu.VMEM((3, 32, 384), BF),
            dma((6,)),
            dma((8,)),
            dma,
            dma((3,)),
            dma((3,)),
            dma,
            dma,
            dma((3, CHUNKS)),
            dma((3, CHUNKS)),
            dma((3,)),
            dma((3,)),
        ],
        compiler_params=pltpu.CompilerParams(
            collective_id=0, has_side_effects=True, vmem_limit_bytes=62 * 1024 * 1024
        ),
    )(
        jnp.transpose(near_send, (0, 2, 1)),
        jnp.transpose(coup_send, (0, 2, 1)),
        near_slot.T,
        coup_slot.T,
        *big,
    )


def solution(mesh):
    placed = (
        P("rhs", "leaf", None),
        P("leaf", "rhs", None, None),
        P("leaf", None, None),
        P("leaf", "rhs"),
        P("leaf", None, None),
        P("leaf", None, None),
        P("leaf", None, "rhs"),
        P("leaf", None, None),
        P("leaf", None, None),
        P("leaf", None, None),
        P("leaf", "rhs"),
    )
    return jax.shard_map(
        functools.partial(shards, mesh.shape["leaf"]),
        mesh=mesh,
        in_specs=placed,
        out_specs=P("rhs", "leaf", None),
        check_vma=False,
    )
```

time: 114 us -> 36.5 us (0.32)
  the two profiles are of different devices: /device:TPU:32 before, /device:TPU:6 now
where the time goes in v1:
time: 36.5 us; the launch traced here: 36.4 us
  Pallas kernels  35 us (96%)
  local copies, waits for them, and re-layouts  1.35 us (4%)
    pallas_call x1, Pallas kernels, shards(): pl.pallas_call(functools.partial(kernel, n_leaf), out_shape=jax.ShapeDtyp...  35 us
    unnamed x1, local copies, waits for them, and re-layouts  1.35 us

profile of v1, /device:TPU:6, one launch (start us, length us, event | category | flops | bytes accessed | tf_op | source)
XLA Modules:
  0.0 36.4 jit_solution(13240144572475531130)
XLA Ops:
  0.0 35.0 %shard_map.109 = bf16[4,8,384]{2,1,0:T(8,128)(2,1)} custom-call(s32[1,1,64]{2,1,0:T(1,128)} %bitcast.6, s32[1,1,64]{2,1,0:T(1,128)} %bitcast.7, s32[4,8]{1,0:T(4,128)} %bitcast.4, s32[4,14]{1,0:T(4,128)} %bitcast.5, bf16[4,8,384]{2,1,0:T(8,128)(2,1)} %density_h.1, bf16[8,4,384,384]{3,2,1,0:T(8,128)(2,1)} %near_h.1, bf16[8,64,384]{2,1,0:T(8,128)(2,1)} %col_h.1, ...), custom_call_target="tpu_custom_call" | custom-call | tf_op jit(solution)/shard_map/pallas_call | solution.py:297
  35.0 1.3 %copy.13 = bf16[4,8,384]{2,1,0:T(8,128)(2,1)} copy(bf16[4,8,384]{2,1,0:T(8,128)(2,1)} %shard_map.109) | data formatting | bytes 49152

commit v2 on v1

v2 whole, which is shorter than its diff:
```python
import functools

import jax
import jax.numpy as jnp
from jax import lax
from jax.experimental import pallas as pl
from jax.experimental.pallas import tpu as pltpu
from jax.sharding import PartitionSpec as P

BF = jnp.bfloat16
F32 = jnp.float32
MESH = pl.DeviceIdType.MESH
NT = (((1,), (1,)), ((), ()))
NN = (((1,), (0,)), ((), ()))
ORDER = (12, 13, 8, 9, 10, 11, 0, 1, 2, 3, 4, 5, 6, 7)
CHUNKS = (2, 4)


def dot(a, b, dims=NN):
    return lax.dot_general(a, b, dims, preferred_element_type=F32)


def iota(shape, axis):
    return lax.broadcasted_iota(jnp.int32, shape, axis)


def kernel(
    n_leaf,
    near_send_h,
    coup_send_h,
    near_slot_h,
    coup_slot_h,
    density_h,
    near_h,
    col_h,
    up_h,
    coupling_h,
    down_h,
    row_h,
    out,
    near_send,
    coup_send,
    near_slot,
    coup_slot,
    density,
    near,
    col,
    up,
    coupling,
    down,
    row,
    slots,
    slots_s,
    tiles,
    charges,
    table_a,
    table_b,
    send1,
    send2,
    recv2,
    send4,
    recv4,
    in_sem,
    near_sem,
    smem_sem,
    s0_send,
    s0_recv,
    s1_send,
    s1_recv,
    s2_send,
    s2_recv,
    s4_send,
    s4_recv,
):
    me = lax.axis_index("leaf")
    y = lax.axis_index("rhs")
    first = (
        (density_h, density),
        (col_h, col),
        (near_send_h, near_send),
        (coup_send_h, coup_send),
        (near_slot_h, near_slot),
        (coup_slot_h, coup_slot),
        (up_h, up),
    )
    later = ((coupling_h, coupling), (down_h, down), (row_h, row))
    loads = [pltpu.make_async_copy(a, b, in_sem.at[i]) for i, (a, b) in enumerate(first + later)]
    for load in loads[:7]:
        load.start()

    barrier = pltpu.get_barrier_semaphore()
    zs = [lax.rem(me // 8 + dz, n_leaf // 8) * 8 for dz in range(n_leaf // 8)]
    xs = [lax.rem(me // 2 % 4 + w // 2, 4) * 2 + lax.rem(me % 2 + w % 2, 2) for w in range(8)]
    far_z = sorted(range(n_leaf // 8), key=lambda dz: -min(dz, n_leaf // 8 - dz))
    far_x = (5, 4, 3, 2, 7, 6, 1, 0)
    for dz, w in [(dz, w) for dz in far_z for w in far_x if dz or w]:
        pl.semaphore_signal(barrier, inc=1, device_id={"leaf": zs[dz] + xs[w]}, device_id_type=MESH)
    for e in range(1, 4):
        pl.semaphore_signal(barrier, inc=1, device_id={"rhs": lax.rem(y + e, 4)}, device_id_type=MESH)

    blocks = [pltpu.make_async_copy(near_h.at[i], near.at[i], near_sem.at[i]) for i in range(8)]
    for load in loads[7:] + blocks:
        load.start()

    for load in loads[:7]:
        load.wait()
    slots[0, :, :] = jnp.zeros((8, 128), jnp.int32)
    slots[0, 0:4, 0:8] = near_slot[...]
    slots[0, 4:8, 0:14] = coup_slot[...]

    flat = density[...].reshape(32, 384)
    stacked = jnp.concatenate([flat[:, 128 * c : 128 * c + 128] for c in range(3)], axis=0)
    r, q = iota((128, 96), 0), iota((128, 96), 1)
    source = r % 4 * 8 + r % 64 // 8
    pick = (r < 64) & (q == source + r // 4 % 2 * 32) | (r >= 64) & (r % 8 < 4) & (q == source + 64)
    tile = dot(jnp.where(pick, 1.0, 0.0).astype(BF), stacked)
    r, q = iota((128, 32), 0), iota((128, 32), 1)
    pick = (r % 16 >= 4) & (r % 16 < 8) & (q == r % 4 * 8 + r // 16)
    low = dot(jnp.where(pick, 1.0, 0.0).astype(BF), flat).astype(BF)
    left = iota((16, 128), 1) < 64

    def twice(a):
        return jnp.concatenate([a, a], axis=0)

    level = [dot(low[16 * i : 16 * i + 16], twice(col[i]), NT) for i in range(8)]
    level_values = [a.astype(BF).astype(F32) for a in level]
    for base, count in ((0, 4), (4, 2)):
        level = [
            dot(
                jnp.where(left, level[2 * j].astype(BF).astype(F32), level[2 * j + 1].astype(BF).astype(F32)).astype(BF),
                twice(up[base + j]),
                NT,
            )
            for j in range(count)
        ]
        level_values += [a.astype(BF).astype(F32) for a in level]
    for i in range(14):
        value = level_values[i][:8]
        charges[i] = value.astype(BF)
        if i < 8:
            tiles[0, i] = tile[8 * i : 8 * i + 8].astype(BF)
            tiles[1, i] = tile[64 + 8 * i : 72 + 8 * i].astype(BF)
            table_a[i] = tile[8 * i : 8 * i + 8].astype(BF)
            value += tile[64 + 8 * i : 72 + 8 * i]
        table_b[i] = value.astype(BF)

    def listed(peer, _):
        leaf = near_send[0, 0, peer]
        send1[0, peer] = tiles[0, leaf]
        send1[1, peer] = tiles[1, leaf] + charges[coup_send[0, 0, peer]]
        return 0

    lax.fori_loop(0, n_leaf, listed, 0, unroll=8)
    pl.semaphore_wait(barrier, n_leaf + 2)

    slot_copies = [
        pltpu.make_async_remote_copy(
            slots.at[0],
            slots.at[e],
            s0_send.at[e - 1],
            s0_recv.at[e - 1],
            device_id={"rhs": lax.rem(y + e, 4)},
            device_id_type=MESH,
        )
        for e in range(1, 4)
    ]
    for copy in slot_copies:
        copy.start()

    tables = ((table_a, 8), (table_b, 14))
    for half, (table, own) in enumerate(tables):
        for dz, w in [(dz, w) for w in far_x for dz in far_z if dz or w]:
            peer = zs[dz] + xs[w]
            pltpu.make_async_remote_copy(
                send1.at[half, peer],
                table.at[own + me],
                s1_send.at[half],
                s1_recv.at[half],
                device_id={"leaf": peer},
                device_id_type=MESH,
            ).start()
        table[own + me] = send1[half, me]

    for copy in slot_copies:
        copy.wait_recv()
    to_smem = pltpu.make_async_copy(slots, slots_s, smem_sem)
    to_smem.start()
    to_smem.wait()

    everything = [
        pltpu.make_async_remote_copy(
            send1.at[half, pl.ds(0, n_leaf - 1)],
            table.at[pl.ds(own, n_leaf - 1)],
            s1_send.at[half],
            s1_recv.at[half],
            device_id={"leaf": lax.rem(me + 1, n_leaf)},
            device_id_type=MESH,
        )
        for half, (table, own) in enumerate(tables)
    ]

    rows, lanes = iota((8, 128), 0), iota((8, 128), 1)
    mask_n = jnp.where(rows < 4, 1.0, 0.0).astype(BF)
    mask_a = jnp.where((rows >= 4) & (lanes < 64), 1.0, 0.0).astype(BF)
    mask_b = jnp.where((rows >= 4) & (lanes >= 64), 1.0, 0.0).astype(BF)

    def read(half, e, i):
        slot = slots_s[e, i % 4, i // 4]
        if half == 0:
            return table_a[slot]
        value = table_b[slot + jnp.where(slot >= 8, 6, 0)] * mask_n
        if i < 28:
            g, k = ORDER[i // 2], i % 2 * 2
            value += table_b[slots_s[e, 4 + k, g]] * mask_a + table_b[slots_s[e, 5 + k, g]] * mask_b
        return value

    sends = [[], []]
    for half in range(2):
        everything[half].wait_recv()
        per = 32 // CHUNKS[half]
        for chunk in range(CHUNKS[half]):
            span = pl.ds(chunk * per, per)
            for e in (2, 1, 3):
                for i in range(chunk * per, chunk * per + per):
                    send2[half, e - 1, i] = read(half, 4 - e, i)
                copy = pltpu.make_async_remote_copy(
                    send2.at[half, e - 1, span],
                    recv2.at[half, e, span],
                    s2_send.at[half, e - 1, chunk],
                    s2_recv.at[half, e - 1, chunk],
                    device_id={"rhs": lax.rem(y + e, 4)},
                    device_id_type=MESH,
                )
                copy.start()
                sends[half].append(copy)
        for i in range(32):
            recv2[half, 0, i] = read(half, 0, i)

    for load in loads[7:]:
        load.wait()

    top = iota((8, 128), 0) < 4

    def regroup(half, i):
        x = [recv2[half, e, i].astype(F32) for e in range(4)]
        z = [pltpu.roll(p, 4, 0) for p in x]
        groups = (
            [jnp.where(top, x[0], z[1]), jnp.where(top, x[2], z[3])],
            [jnp.where(top, z[0], x[1]), jnp.where(top, z[2], x[3])],
        )
        return [jnp.concatenate(g, axis=0).astype(BF) for g in groups]

    total = []
    for chunk in range(CHUNKS[0]):
        for copy in sends[0][3 * chunk : 3 * chunk + 3]:
            copy.wait_recv()
        for leaf in range(chunk * 8 // CHUNKS[0], (chunk + 1) * 8 // CHUNKS[0]):
            blocks[leaf].wait()
            value = None
            for k in range(4):
                part = dot(jnp.concatenate(regroup(0, 4 * leaf + k), axis=1), near[leaf, k, :, 0:256], NT)
                value = part if value is None else value + part
            total.append(value)

    field = {}
    for chunk in range(CHUNKS[1]):
        for copy in sends[1][3 * chunk : 3 * chunk + 3]:
            copy.wait_recv()
        pairs = {}
        for leaf in range(chunk * 8 // CHUNKS[1], (chunk + 1) * 8 // CHUNKS[1]):
            for k in (0, 2):
                one, two = regroup(1, 4 * leaf + k), regroup(1, 4 * leaf + k + 1)
                pairs[4 * leaf + k], pairs[4 * leaf + k + 1] = one[1], two[1]
                total[leaf] += dot(
                    jnp.concatenate([one[0], two[0]], axis=1),
                    jnp.concatenate([near[leaf, k, :, 256:384], near[leaf, k + 1, :, 256:384]], axis=1),
                    NT,
                )
        for i in pairs:
            if i < 28 and i % 2 == 0:
                g = ORDER[i // 2]
                field[g] = dot(jnp.concatenate([pairs[i], pairs[i + 1]], axis=1), coupling[g], NT)

    def gain(parent, index):
        return dot(field[parent].astype(BF), down[index])

    for base, children, count, first in ((12, 8, 2, 4), (8, 0, 4, 0)):
        for j in range(count):
            both = gain(base + j, first + j)
            field[children + 2 * j] += both[:, :64]
            field[children + 2 * j + 1] += both[:, 64:]
    whole = jnp.concatenate(
        [(total[i] + dot(field[i].astype(BF), row[i])).astype(BF) for i in range(8)], axis=0
    )
    r, q = iota((128, 128), 0), iota((128, 128), 1)
    pick = q == r % 8 * 16 + r // 32 * 4 + r // 8 % 4
    sorted_rows = dot(jnp.where(pick, 1.0, 0.0).astype(BF), whole)
    last = []
    for e in range(1, 4):
        send4[e - 1] = sorted_rows[32 * e : 32 * e + 32].astype(BF)
        copy = pltpu.make_async_remote_copy(
            send4.at[e - 1],
            recv4.at[3 - e],
            s4_send.at[e - 1],
            s4_recv.at[3 - e],
            device_id={"rhs": lax.rem(y + 4 - e, 4)},
            device_id_type=MESH,
        )
        copy.start()
        last.append(copy)
    for copy in last:
        copy.wait()
    result = sorted_rows[:32]
    for e in range(3):
        result += recv4[e].astype(F32)
    out[...] = result.astype(BF).reshape(4, 8, 384)

    for copy in slot_copies:
        copy.wait_send()
    for copy in everything + sends[0] + sends[1]:
        copy.wait_send()


def shards(n_leaf, density, near_blocks, near_send, near_slot, col, up, coupling, down, row, coup_send, coup_slot):
    vmem = pl.BlockSpec(memory_space=pltpu.VMEM)
    hbm = pl.BlockSpec(memory_space=pl.ANY)
    big = [density, near_blocks, col, up, coupling, down, row]
    dma = pltpu.SemaphoreType.DMA
    return pl.pallas_call(
        functools.partial(kernel, n_leaf),
        out_shape=jax.ShapeDtypeStruct((4, 8, 384), BF),
        in_specs=[hbm] * (4 + len(big)),
        out_specs=vmem,
        scratch_shapes=[
            pltpu.SMEM((1, 1, n_leaf), jnp.int32),
            pltpu.SMEM((1, 1, n_leaf), jnp.int32),
            pltpu.VMEM((4, 8), jnp.int32),
            pltpu.VMEM((4, 14), jnp.int32),
        ]
        + [pltpu.VMEM(a.shape, a.dtype) for a in big]
        + [
            pltpu.VMEM((4, 8, 128), jnp.int32),
            pltpu.SMEM((4, 8, 128), jnp.int32),
            pltpu.VMEM((2, 8, 8, 128), BF),
            pltpu.VMEM((14, 8, 128), BF),
            pltpu.VMEM((8 + n_leaf, 8, 128), BF),
            pltpu.VMEM((14 + n_leaf, 8, 128), BF),
            pltpu.VMEM((2, n_leaf, 8, 128), BF),
            pltpu.VMEM((2, 3, 32, 8, 128), BF),
            pltpu.VMEM((2, 4, 32, 8, 128), BF),
            pltpu.VMEM((3, 32, 384), BF),
            pltpu.VMEM((3, 32, 384), BF),
            dma((10,)),
            dma((8,)),
            dma,
            dma((3,)),
            dma((3,)),
            dma((2,)),
            dma((2,)),
            dma((2, 3, max(CHUNKS))),
            dma((2, 3, max(CHUNKS))),
            dma((3,)),
            dma((3,)),
        ],
        compiler_params=pltpu.CompilerParams(
            collective_id=0, has_side_effects=True, vmem_limit_bytes=62 * 1024 * 1024
        ),
    )(
        jnp.transpose(near_send, (0, 2, 1)),
        jnp.transpose(coup_send, (0, 2, 1)),
        near_slot.T,
        coup_slot.T,
        *big,
    )


def solution(mesh):
    placed = (
        P("rhs", "leaf", None),
        P("leaf", "rhs", None, None),
        P("leaf", None, None),
        P("leaf", "rhs"),
        P("leaf", None, None),
        P("leaf", None, None),
        P("leaf", None, "rhs"),
        P("leaf", None, None),
        P("leaf", None, None),
        P("leaf", None, None),
        P("leaf", "rhs"),
    )
    return jax.shard_map(
        functools.partial(shards, mesh.shape["leaf"]),
        mesh=mesh,
        in_specs=placed,
        out_specs=P("rhs", "leaf", None),
        check_vma=False,
    )
```

time: 36.5 us -> 32.2 us (0.88)
  the two profiles are of different devices: /device:TPU:6 before, /device:TPU:32 now
where the time goes in v2:
time: 32.2 us; the launch traced here: 32.1 us
  Pallas kernels  30.7 us (95%)
  local copies, waits for them, and re-layouts  1.35 us (4%)
    pallas_call x1, Pallas kernels, shards(): pl.pallas_call(functools.partial(kernel, n_leaf), out_shape=jax.ShapeDtyp...  30.7 us
    unnamed x1, local copies, waits for them, and re-layouts  1.35 us

profile of v2, /device:TPU:32, one launch (start us, length us, event | category | flops | bytes accessed | tf_op | source)
XLA Modules:
  0.0 32.1 jit_solution(12893282779035657614)
XLA Ops:
  0.0 30.7 %shard_map.109 = bf16[4,8,384]{2,1,0:T(8,128)(2,1)} custom-call(s32[1,1,64]{2,1,0:T(1,128)} %bitcast.6, s32[1,1,64]{2,1,0:T(1,128)} %bitcast.7, s32[4,8]{1,0:T(4,128)} %bitcast.4, s32[4,14]{1,0:T(4,128)} %bitcast.5, bf16[4,8,384]{2,1,0:T(8,128)(2,1)} %density_h.1, bf16[8,4,384,384]{3,2,1,0:T(8,128)(2,1)} %near_h.1, bf16[8,64,384]{2,1,0:T(8,128)(2,1)} %col_h.1, ...), custom_call_target="tpu_custom_call" | custom-call | tf_op jit(solution)/shard_map/pallas_call | solution.py:329
  30.7 1.3 %copy.13 = bf16[4,8,384]{2,1,0:T(8,128)(2,1)} copy(bf16[4,8,384]{2,1,0:T(8,128)(2,1)} %shard_map.109) | data formatting | bytes 49152

commit v3 on v2

--- a/solution.py
+++ b/solution.py
@@ -13,7 +13,7 @@
 NT = (((1,), (1,)), ((), ()))
 NN = (((1,), (0,)), ((), ()))
 ORDER = (12, 13, 8, 9, 10, 11, 0, 1, 2, 3, 4, 5, 6, 7)
-CHUNKS = (2, 4)
+CHUNKS = (2, 2)
 
 
 def dot(a, b, dims=NN):
@@ -112,7 +112,7 @@
     stacked = jnp.concatenate([flat[:, 128 * c : 128 * c + 128] for c in range(3)], axis=0)
     r, q = iota((128, 96), 0), iota((128, 96), 1)
     source = r % 4 * 8 + r % 64 // 8
-    pick = (r < 64) & (q == source + r // 4 % 2 * 32) | (r >= 64) & (r % 8 < 4) & (q == source + 64)
+    pick = (r < 64) & (r % 8 < 4) & (q == source) | (r >= 64) & (q == source + 32 + r // 4 % 2 * 32)
     tile = dot(jnp.where(pick, 1.0, 0.0).astype(BF), stacked)
     r, q = iota((128, 32), 0), iota((128, 32), 1)
     pick = (r % 16 >= 4) & (r % 16 < 8) & (q == r % 4 * 8 + r // 16)
@@ -140,14 +140,14 @@
         if i < 8:
             tiles[0, i] = tile[8 * i : 8 * i + 8].astype(BF)
             tiles[1, i] = tile[64 + 8 * i : 72 + 8 * i].astype(BF)
-            table_a[i] = tile[8 * i : 8 * i + 8].astype(BF)
-            value += tile[64 + 8 * i : 72 + 8 * i]
-        table_b[i] = value.astype(BF)
+            table_b[i] = tile[64 + 8 * i : 72 + 8 * i].astype(BF)
+            value += tile[8 * i : 8 * i + 8]
+        table_a[i] = value.astype(BF)
 
     def listed(peer, _):
         leaf = near_send[0, 0, peer]
-        send1[0, peer] = tiles[0, leaf]
-        send1[1, peer] = tiles[1, leaf] + charges[coup_send[0, 0, peer]]
+        send1[0, peer] = tiles[0, leaf] + charges[coup_send[0, 0, peer]]
+        send1[1, peer] = tiles[1, leaf]
         return 0
 
     lax.fori_loop(0, n_leaf, listed, 0, unroll=8)
@@ -167,7 +167,7 @@
     for copy in slot_copies:
         copy.start()
 
-    tables = ((table_a, 8), (table_b, 14))
+    tables = ((table_a, 14), (table_b, 8))
     for half, (table, own) in enumerate(tables):
         for dz, w in [(dz, w) for w in far_x for dz in far_z if dz or w]:
             peer = zs[dz] + xs[w]
@@ -206,12 +206,12 @@
 
     def read(half, e, i):
         slot = slots_s[e, i % 4, i // 4]
-        if half == 0:
-            return table_a[slot]
-        value = table_b[slot + jnp.where(slot >= 8, 6, 0)] * mask_n
+        if half == 1:
+            return table_b[slot]
+        value = table_a[slot + jnp.where(slot >= 8, 6, 0)] * mask_n
         if i < 28:
             g, k = ORDER[i // 2], i % 2 * 2
-            value += table_b[slots_s[e, 4 + k, g]] * mask_a + table_b[slots_s[e, 5 + k, g]] * mask_b
+            value += table_a[slots_s[e, 4 + k, g]] * mask_a + table_a[slots_s[e, 5 + k, g]] * mask_b
         return value
 
     sends = [[], []]
@@ -220,7 +220,7 @@
         per = 32 // CHUNKS[half]
         for chunk in range(CHUNKS[half]):
             span = pl.ds(chunk * per, per)
-            for e in (2, 1, 3):
+            for e in (1, 3, 2):
                 for i in range(chunk * per, chunk * per + per):
                     send2[half, e - 1, i] = read(half, 4 - e, i)
                 copy = pltpu.make_async_remote_copy(
@@ -250,48 +250,45 @@
         )
         return [jnp.concatenate(g, axis=0).astype(BF) for g in groups]
 
-    total = []
+    def arrived(half, chunk):
+        for copy in sends[half][3 * chunk : 3 * chunk + 3]:
+            copy.wait_recv()
+        return range(chunk * 8 // CHUNKS[half], (chunk + 1) * 8 // CHUNKS[half])
+
+    pairs, total = {}, []
     for chunk in range(CHUNKS[0]):
-        for copy in sends[0][3 * chunk : 3 * chunk + 3]:
-            copy.wait_recv()
-        for leaf in range(chunk * 8 // CHUNKS[0], (chunk + 1) * 8 // CHUNKS[0]):
+        for leaf in arrived(0, chunk):
             blocks[leaf].wait()
             value = None
-            for k in range(4):
-                part = dot(jnp.concatenate(regroup(0, 4 * leaf + k), axis=1), near[leaf, k, :, 0:256], NT)
+            for k in (0, 2):
+                one, two = regroup(0, 4 * leaf + k), regroup(0, 4 * leaf + k + 1)
+                pairs[4 * leaf + k], pairs[4 * leaf + k + 1] = one[1], two[1]
+                part = dot(
+                    jnp.concatenate([one[0], two[0]], axis=1),
+                    jnp.concatenate([near[leaf, k, :, 0:128], near[leaf, k + 1, :, 0:128]], axis=1),
+                    NT,
+                )
                 value = part if value is None else value + part
             total.append(value)
 
     field = {}
-    for chunk in range(CHUNKS[1]):
-        for copy in sends[1][3 * chunk : 3 * chunk + 3]:
-            copy.wait_recv()
-        pairs = {}
-        for leaf in range(chunk * 8 // CHUNKS[1], (chunk + 1) * 8 // CHUNKS[1]):
-            for k in (0, 2):
-                one, two = regroup(1, 4 * leaf + k), regroup(1, 4 * leaf + k + 1)
-                pairs[4 * leaf + k], pairs[4 * leaf + k + 1] = one[1], two[1]
-                total[leaf] += dot(
-                    jnp.concatenate([one[0], two[0]], axis=1),
-                    jnp.concatenate([near[leaf, k, :, 256:384], near[leaf, k + 1, :, 256:384]], axis=1),
-                    NT,
-                )
-        for i in pairs:
-            if i < 28 and i % 2 == 0:
-                g = ORDER[i // 2]
-                field[g] = dot(jnp.concatenate([pairs[i], pairs[i + 1]], axis=1), coupling[g], NT)
-
-    def gain(parent, index):
-        return dot(field[parent].astype(BF), down[index])
-
+    for j, g in enumerate(ORDER):
+        field[g] = dot(jnp.concatenate([pairs[2 * j], pairs[2 * j + 1]], axis=1), coupling[g], NT)
     for base, children, count, first in ((12, 8, 2, 4), (8, 0, 4, 0)):
         for j in range(count):
-            both = gain(base + j, first + j)
+            both = dot(field[base + j].astype(BF), down[first + j])
             field[children + 2 * j] += both[:, :64]
             field[children + 2 * j + 1] += both[:, 64:]
-    whole = jnp.concatenate(
-        [(total[i] + dot(field[i].astype(BF), row[i])).astype(BF) for i in range(8)], axis=0
-    )
+    for i in range(8):
+        total[i] += dot(field[i].astype(BF), row[i])
+
+    for chunk in range(CHUNKS[1]):
+        for leaf in arrived(1, chunk):
+            for k in range(4):
+                total[leaf] += dot(
+                    jnp.concatenate(regroup(1, 4 * leaf + k), axis=1), near[leaf, k, :, 128:384], NT
+                )
+    whole = jnp.concatenate([value.astype(BF) for value in total], axis=0)
     r, q = iota((128, 128), 0), iota((128, 128), 1)
     pick = q == r % 8 * 16 + r // 32 * 4 + r // 8 % 4
     sorted_rows = dot(jnp.where(pick, 1.0, 0.0).astype(BF), whole)
@@ -343,8 +340,8 @@
             pltpu.SMEM((4, 8, 128), jnp.int32),
             pltpu.VMEM((2, 8, 8, 128), BF),
             pltpu.VMEM((14, 8, 128), BF),
+            pltpu.VMEM((14 + n_leaf, 8, 128), BF),
             pltpu.VMEM((8 + n_leaf, 8, 128), BF),
-            pltpu.VMEM((14 + n_leaf, 8, 128), BF),
             pltpu.VMEM((2, n_leaf, 8, 128), BF),
             pltpu.VMEM((2, 3, 32, 8, 128), BF),
             pltpu.VMEM((2, 4, 32, 8, 128), BF),

time: 32.2 us -> 31.8 us (0.988)
  Pallas kernels: 30.7 us -> 30.3 us
    pallas_call x1, Pallas kernels: 30.7 us -> 30.3 us  [shards(): pl.pallas_call(functools.partial(kernel, n_leaf), out_shape=jax.ShapeDtyp...]
where the time goes in v3:
time: 31.8 us; the launch traced here: 31.6 us
  Pallas kernels  30.3 us (95%)
  local copies, waits for them, and re-layouts  1.35 us (4%)
    pallas_call x1, Pallas kernels, shards(): pl.pallas_call(functools.partial(kernel, n_leaf), out_shape=jax.ShapeDtyp...  30.3 us
    unnamed x1, local copies, waits for them, and re-layouts  1.35 us

profile of v3, /device:TPU:32, one launch (start us, length us, event | category | flops | bytes accessed | tf_op | source)
XLA Modules:
  0.0 31.6 jit_solution(7724746246524862295)
XLA Ops:
  0.0 30.3 %shard_map.109 = bf16[4,8,384]{2,1,0:T(8,128)(2,1)} custom-call(s32[1,1,64]{2,1,0:T(1,128)} %bitcast.6, s32[1,1,64]{2,1,0:T(1,128)} %bitcast.7, s32[4,8]{1,0:T(4,128)} %bitcast.4, s32[4,14]{1,0:T(4,128)} %bitcast.5, bf16[4,8,384]{2,1,0:T(8,128)(2,1)} %density_h.1, bf16[8,4,384,384]{3,2,1,0:T(8,128)(2,1)} %near_h.1, bf16[8,64,384]{2,1,0:T(8,128)(2,1)} %col_h.1, ...), custom_call_target="tpu_custom_call" | custom-call | tf_op jit(solution)/shard_map/pallas_call | solution.py:326
  30.3 1.3 %copy.13 = bf16[4,8,384]{2,1,0:T(8,128)(2,1)} copy(bf16[4,8,384]{2,1,0:T(8,128)(2,1)} %shard_map.109) | data formatting | bytes 49152

commit v4 on v3

--- a/solution.py
+++ b/solution.py
@@ -169,7 +169,7 @@
 
     tables = ((table_a, 14), (table_b, 8))
     for half, (table, own) in enumerate(tables):
-        for dz, w in [(dz, w) for w in far_x for dz in far_z if dz or w]:
+        for dz, w in [(dz, w) for w in (far_x, far_x[::-1])[half] for dz in far_z if dz or w]:
             peer = zs[dz] + xs[w]
             pltpu.make_async_remote_copy(
                 send1.at[half, peer],
@@ -293,7 +293,7 @@
     pick = q == r % 8 * 16 + r // 32 * 4 + r // 8 % 4
     sorted_rows = dot(jnp.where(pick, 1.0, 0.0).astype(BF), whole)
     last = []
-    for e in range(1, 4):
+    for e in (2, 1, 3):
         send4[e - 1] = sorted_rows[32 * e : 32 * e + 32].astype(BF)
         copy = pltpu.make_async_remote_copy(
             send4.at[e - 1],

time: 31.8 us -> 31.6 us (level)
  no operation moved by 1% of the time
where the time goes in v4:
time: 31.6 us; the launch traced here: 31.5 us
  Pallas kernels  30.1 us (95%)
  local copies, waits for them, and re-layouts  1.35 us (4%)
    pallas_call x1, Pallas kernels, shards(): pl.pallas_call(functools.partial(kernel, n_leaf), out_shape=jax.ShapeDtyp...  30.1 us
    unnamed x1, local copies, waits for them, and re-layouts  1.35 us

profile of v4, /device:TPU:32, one launch (start us, length us, event | category | flops | bytes accessed | tf_op | source)
XLA Modules:
  0.0 31.5 jit_solution(4555705880301458349)
XLA Ops:
  0.0 30.1 %shard_map.109 = bf16[4,8,384]{2,1,0:T(8,128)(2,1)} custom-call(s32[1,1,64]{2,1,0:T(1,128)} %bitcast.6, s32[1,1,64]{2,1,0:T(1,128)} %bitcast.7, s32[4,8]{1,0:T(4,128)} %bitcast.4, s32[4,14]{1,0:T(4,128)} %bitcast.5, bf16[4,8,384]{2,1,0:T(8,128)(2,1)} %density_h.1, bf16[8,4,384,384]{3,2,1,0:T(8,128)(2,1)} %near_h.1, bf16[8,64,384]{2,1,0:T(8,128)(2,1)} %col_h.1, ...), custom_call_target="tpu_custom_call" | custom-call | tf_op jit(solution)/shard_map/pallas_call | solution.py:326
  30.1 1.3 %copy.13 = bf16[4,8,384]{2,1,0:T(8,128)(2,1)} copy(bf16[4,8,384]{2,1,0:T(8,128)(2,1)} %shard_map.109) | data formatting | bytes 49152
